TPU v7x, 256 devices: a whole 4x4x8 slice. The times are simulated.
256 devices in a mesh: seq: 32 (over z, y), mp: 8 (over x, core).
Axes of the slice: x: 4, y: 4, z: 8, core: 2. Of those that a mesh axis runs over, the one named last changes fastest.
Arguments:
- tokens: bfloat16 [49152, 2048], P('seq', 'mp'), may hold values from -12 to 12
- cluster_ids: int32 [49152, 1], P('seq'), may hold values from 0 to 63, as said below
- w_query: bfloat16 [2048, 2048], P(None, 'mp'), may hold values from -0.125 to 0.125
- w_value: bfloat16 [2048, 2048], P(None, 'mp'), may hold values from -0.125 to 0.125
- w_out: bfloat16 [2048, 2048], P('mp'), may hold values from -0.125 to 0.125
Outputs:
- mixed: bfloat16 [49152, 2048], P('seq', 'mp')
Inputs may be any that keep to these rules, and one draw needn't show every extreme that they name: `cluster_ids`: in the rows of one index of seq, no cluster holds more than 48 tokens, and some cluster holds exactly 48.
All inputs are finite; a program needn't handle non-finite values.
Results may differ from a plain program's by a relative error of at most 0.0062.
Values may be sent and summed in bfloat16 or wider, within the bound.
A program may use at most 128 MiB of HBM per device.

v0:
```python
import functools

import jax
import jax.numpy as jnp
import numpy as np
from jax import lax
from jax.experimental import pallas as pl
from jax.experimental.pallas import tpu as pltpu
from jax.sharding import PartitionSpec as P

HD = 128
CAP = 48
NZ, NY, NX = 8, 4, 4
NSEQ = NZ * NY
NMP = 2 * NX
TOK = 1536
GROUPS = 4
BLK = 256
NEG = -1e30
MESH = pl.DeviceIdType.MESH
BF = jnp.bfloat16
F32 = jnp.float32
I32 = jnp.int32
FOLD = np.float32(1.4426950408889634 / np.sqrt(128.0))


def peer_of(s, r, sign):
    g, hi, dy = r // 8, (r // 4) % 2, r % 4
    minus = jnp.where(g == 0, 4, NZ - g)
    dz = jnp.where(hi == 0, g, minus)
    z, y = s // NY, s % NY
    return ((z + sign * dz + NZ) % NZ) * NY + (y + sign * dy + NY) % NY


def rank_of(cluster):
    return (cluster & 1) * NSEQ + (cluster >> 1)


def first_row(rank, s, caps):
    z, y = s // NY, s % NY
    owner, o = rank & (NSEQ - 1), rank >> 5
    dz = ((owner >> 2) - z) & (NZ - 1)
    dy = ((owner & 3) - y) & (NY - 1)
    hi = dz >> 2
    g = jnp.where(hi == 1, (NZ - dz) & 3, dz)
    r = g * 8 + hi * 4 + dy
    return jnp.where(o == 0, r * caps[0], NSEQ * caps[0] + r * caps[1])


class Ring:
    def __init__(self, chunks, s, m, ssem, rsem):
        self.chunks, self.s, self.m = chunks, s, m
        self.ssem, self.rsem = ssem, rsem
        x, c = m // 2, m % 2
        self.right = ((x + 1) % NX) * 2 + c
        self.left = ((x + NX - 1) % NX) * 2 + c
        self.far = ((x + 2) % NX) * 2 + c
        self.sib = x * 2 + 1 - c

    def _copy(self, kind, k, block, to, half=None):
        G, p = self.chunks[k]
        ref = G.at[block, p]
        if half is not None:
            h = G.shape[2] // 2
            ref = G.at[block, p, pl.ds(half * h, h)]
        return pltpu.make_async_remote_copy(
            src_ref=ref,
            dst_ref=ref,
            send_sem=self.ssem.at[kind, k],
            recv_sem=self.rsem.at[kind, k],
            device_id=(self.s, to),
            device_id_type=MESH,
        )

    def send(self, i, k):
        block, to, half = (
            (self.m, self.right, None),
            (self.m, self.left, None),
            (self.m, self.sib, None),
            (self.left, self.right, 0),
            (self.right, self.left, 1),
            (self.left, self.sib, None),
            (self.right, self.sib, None),
            (self.far, self.sib, None),
        )[i]
        return self._copy(i, k, block, to, half)

    def arrival(self, i, k):
        other = lambda block: (block // 2) * 2 + 1 - block % 2
        block, half = (
            (self.left, None),
            (self.right, None),
            (self.sib, None),
            (self.far, 0),
            (self.far, 1),
            (other(self.left), None),
            (other(self.right), None),
            (other(self.far), None),
        )[i]
        return self._copy(i, k, block, self.sib, half)

    def step(self, t, ready, compute):
        n = len(self.chunks)
        if t < n:
            ready(t)
            for i in (0, 1, 2):
                self.send(i, t).start()
        if 1 <= t <= n:
            k = t - 1
            self.arrival(0, k).wait_recv()
            self.send(3, k).start()
            self.send(5, k).start()
            self.arrival(1, k).wait_recv()
            self.send(4, k).start()
            self.send(6, k).start()
        if 2 <= t <= n + 1:
            k = t - 2
            self.arrival(3, k).wait_recv()
            self.arrival(4, k).wait_recv()
            self.send(7, k).start()
        if 3 <= t:
            k = t - 3
            for i in (2, 5, 6, 7):
                self.arrival(i, k).wait_recv()
            compute(k)

    def drain(self):
        for k in range(len(self.chunks)):
            for i in range(8):
                self.send(i, k).wait_send()


def layer_kernel(
    tok_ref, row_ref, col_ref, wq_hbm, wv_hbm, wo_hbm,
    out_ref,
    wq, wv, wo, wcol, buf0, buf1, G0, G1, q0, q1, v0, v1, bias0, bias1,
    att0, att1, back0, back1, G2, cnt, onehot, drow, dcol,
    lsem, ssem1, rsem1, ssem2, rsem2, dsend, drecv, csend, crecv,
    bsend, brecv, wsend, wrecv,
    *, caps,
):
    s, m = lax.axis_index("seq"), lax.axis_index("mp")
    bufs, Gs, qs, vs = (buf0, buf1), (G0, G1), (q0, q1), (v0, v1)
    biases, atts, backs = (bias0, bias1), (att0, att1), (back0, back1)
    spans = (NSEQ * caps[0], NSEQ * caps[1])

    loads = [
        pltpu.make_async_copy(a, b, lsem.at[i])
        for i, (a, b) in enumerate(((wq_hbm, wq), (wv_hbm, wv), (wo_hbm, wo)))
    ]
    for one in loads:
        one.start()

    barrier = pltpu.get_barrier_semaphore()

    def hello(r, carry):
        pl.semaphore_signal(
            barrier, inc=1, device_id=(peer_of(s, r, 1), m), device_id_type=MESH
        )
        return carry

    lax.fori_loop(1, NSEQ, hello, 0)
    for i in range(1, NMP):
        pl.semaphore_signal(
            barrier, inc=1, device_id=(s, lax.rem(m + i, NMP)), device_id_type=MESH
        )

    ids = row_ref[...]
    onehot[...] = (lax.broadcasted_iota(I32, (128, TOK), 0) == ids).astype(F32).astype(BF)
    i0 = lax.broadcasted_iota(I32, (BLK, BLK), 0)
    i1 = lax.broadcasted_iota(I32, (BLK, BLK), 1)
    upper = (i0 < i1).astype(F32).astype(BF)
    seen = first_row(rank_of(lax.broadcasted_iota(I32, (128, 1), 0)), s, caps).astype(F32)
    for b in range(TOK // BLK):
        part = onehot[:, b * BLK:(b + 1) * BLK]
        wide = part.astype(F32)
        ahead = jnp.dot(part, upper, preferred_element_type=F32) + seen
        drow[:, b * BLK:(b + 1) * BLK] = jnp.sum(ahead * wide, axis=0, keepdims=True).astype(I32)
        seen = seen + jnp.sum(wide, axis=1, keepdims=True)
    cnt[0] = lax.dot_general(
        jnp.ones((8, TOK), BF), onehot[...], (((1,), (1,)), ((), ())),
        preferred_element_type=F32,
    )
    pl.semaphore_wait(barrier, NSEQ - 1 + NMP - 1)

    def whole(ref, sem_s, sem_r):
        return pltpu.make_async_remote_copy(
            src_ref=ref, dst_ref=ref, send_sem=sem_s, recv_sem=sem_r,
            device_id=(s, m), device_id_type=MESH,
        )

    def block_copy(o, g, j):
        at = pl.ds(pl.multiple_of(j * caps[o], 16), caps[o])
        return pltpu.make_async_remote_copy(
            src_ref=bufs[o].at[g, at],
            dst_ref=Gs[o].at[m, g, at],
            send_sem=dsend.at[o * GROUPS + g],
            recv_sem=drecv.at[o * GROUPS + g],
            device_id=(peer_of(s, g * 8 + j, 1), m),
            device_id_type=MESH,
        )

    def landed(o, g, ref):
        if g == 0:
            ref = ref.at[pl.ds(caps[o], 7 * caps[o])]
        return whole(ref, dsend.at[o * GROUPS + g], drecv.at[o * GROUPS + g])

    def scatter(o, g):
        n = 8 * caps[o]
        base = o * spans[0] + g * n
        row = lax.broadcasted_iota(I32, (n, TOK), 0) + base
        pick = (row == drow[...]).astype(F32).astype(BF)
        rows = jnp.dot(pick, tok_ref[...], preferred_element_type=F32).astype(BF)
        bufs[o][g] = rows
        if g == 0:
            Gs[o][m, 0, 0:caps[o]] = rows[0:caps[o]]

        def send(j, carry):
            block_copy(o, g, j).start()
            return carry

        lax.fori_loop(1 if g == 0 else 0, 8, send, 0)

    order = [(o, g) for o in range(2) for g in (1, 2, 3, 0)]
    for o, g in order[:GROUPS]:
        scatter(o, g)

    def count_copy(r):
        return pltpu.make_async_remote_copy(
            src_ref=cnt.at[0], dst_ref=cnt.at[r], send_sem=csend, recv_sem=crecv,
            device_id=(peer_of(s, r, 1), m), device_id_type=MESH,
        )

    def send_count(r, carry):
        count_copy(r).start()
        return carry

    def ready(t):
        o, g = order[t]
        landed(o, g, Gs[o].at[m, g]).wait_recv()

    def project(k):
        o, g = order[k]
        if k == 0:
            loads[0].wait()
            loads[1].wait()
            for o2 in range(2):
                for h in range(2):
                    vs[o2][:, h * 256 + HD:(h + 1) * 256] = jnp.ones((spans[o2], HD), BF)
        cap = caps[o]
        rows = jnp.concatenate([Gs[o][i, g] for i in range(NMP)], axis=1)
        query = jnp.dot(rows, wq[...], preferred_element_type=F32).astype(BF)
        value = jnp.dot(rows, wv[...], preferred_element_type=F32).astype(BF)
        for j in range(8):
            at = pl.ds(pl.multiple_of(peer_of(s, g * 8 + j, -1) * cap, 16), cap)
            qs[o][at] = query[j * cap:(j + 1) * cap]
            for h in range(2):
                vs[o][at, h * 256:h * 256 + HD] = value[j * cap:(j + 1) * cap, h * HD:(h + 1) * HD]

    def masks():
        whole(cnt.at[pl.ds(1, NSEQ - 1)], csend, crecv).wait_recv()
        tall = cnt[:, 0, :]
        for o in range(2):
            shape = (NSEQ, spans[o])
            r = lax.broadcasted_iota(I32, shape, 0)
            g, hi, dy = r >> 3, (r >> 2) & 1, r & 3
            dz = jnp.where(hi == 0, g, jnp.where(g == 0, 4, NZ - g))
            src = (((s // NY) - dz) & (NZ - 1)) * NY + (((s % NY) - dy) & (NY - 1))
            off = lax.broadcasted_iota(I32, shape, 1) - src * caps[o]
            mine = rank_of(lax.broadcasted_iota(I32, (NSEQ, 128), 1)) == NSEQ * o + s
            have = jnp.sum(jnp.where(mine, tall, 0.0), axis=1, keepdims=True)
            held = jnp.where((off >= 0) & (off.astype(F32) < have), 1.0, 0.0)
            held = jnp.sum(held, axis=0, keepdims=True)
            biases[o][...] = jnp.broadcast_to((1.0 - held) * NEG, (8, spans[o]))

    def columns():
        cl = lax.broadcasted_iota(I32, (BLK, 128), 1)
        lower = (i1 < i0).astype(F32).astype(BF)
        past = first_row(rank_of(lax.broadcasted_iota(I32, (1, 128), 1)), s, caps).astype(F32)
        for b in range(TOK // BLK):
            wide = (cl == col_ref[b * BLK:(b + 1) * BLK]).astype(F32)
            ahead = jnp.dot(lower, wide.astype(BF), preferred_element_type=F32) + past
            dcol[b * BLK:(b + 1) * BLK, :] = jnp.sum(ahead * wide, axis=1, keepdims=True).astype(I32)
            past = past + jnp.sum(wide, axis=0, keepdims=True)

    def attend(o, i):
        lo, hi = i * BLK, (i + 1) * BLK
        dims = (((1,), (1,)), ((), ()))
        below = i0 >= i1

        def head(h, carry):
            lanes = pl.ds(pl.multiple_of(h * HD, HD), HD)
            query = qs[o][lo:hi, lanes]
            bias = biases[o][0:1, :]
            near = lax.dot_general(query, query, dims, preferred_element_type=F32) * FOLD
            near = jnp.where(below, near + bias[:, lo:hi], NEG)
            scores = near
            if i:
                keys = qs[o][0:lo, lanes]
                past = lax.dot_general(query, keys, dims, preferred_element_type=F32) * FOLD
                scores = jnp.concatenate([past + bias[:, :lo], near], axis=1)
            top = jnp.max(scores, axis=1, keepdims=True)
            expo = jnp.exp2(scores - top).astype(BF)
            values = vs[o][0:hi, pl.ds(pl.multiple_of(h * 256, 256), 256)]
            got = jnp.dot(expo, values, preferred_element_type=F32)
            atts[o][lo:hi, lanes] = (got[:, :HD] / got[:, HD:HD + 1]).astype(BF)
            return carry

        lax.fori_loop(0, 2, head, 0)

    def back_copy(o, r):
        src = peer_of(s, r, -1)
        return pltpu.make_async_remote_copy(
            src_ref=atts[o].at[pl.ds(pl.multiple_of(src * caps[o], 16), caps[o])],
            dst_ref=backs[o].at[pl.ds(pl.multiple_of(r * caps[o], 16), caps[o])],
            send_sem=bsend.at[o],
            recv_sem=brecv.at[o],
            device_id=(src, m),
            device_id_type=MESH,
        )

    def give_back(o):
        def send(r, carry):
            back_copy(o, r).start()
            return carry

        lax.fori_loop(1, NSEQ, send, 0)
        backs[o][0:caps[o]] = atts[o][pl.ds(pl.multiple_of(s * caps[o], 16), caps[o])]

    def returned(o):
        ref = backs[o].at[pl.ds(caps[o], (NSEQ - 1) * caps[o])]
        return whole(ref, bsend.at[o], brecv.at[o])

    ring = Ring([(Gs[o], g) for o, g in order], s, m, ssem1, rsem1)
    for t in range(2 * GROUPS + 3):
        ring.step(t, ready, project)
        if t < 2:
            scatter(*order[GROUPS + 2 * t])
            scatter(*order[GROUPS + 2 * t + 1])
        if t == 1:
            lax.fori_loop(1, NSEQ, send_count, 0)
        if t == 6:
            masks()
            attend(0, 0)
            attend(0, 1)
            attend(0, 2)
        if t == 7:
            attend(0, 3)
            attend(0, 4)
        if t == 8:
            attend(0, 5)
            give_back(0)
    for i in range(spans[1] // BLK):
        attend(1, i)
    give_back(1)

    loads[2].wait()

    def wcopy(i, block, to):
        return pltpu.make_async_remote_copy(
            src_ref=wo.at[:, pl.ds(pl.multiple_of(to * 256, 256), 256)],
            dst_ref=wcol.at[block],
            send_sem=wsend.at[i],
            recv_sem=wrecv.at[i],
            device_id=(s, to),
            device_id_type=MESH,
        )

    for i in range(1, NMP):
        wcopy(i, m, lax.rem(m + i, NMP)).start()
    wcol[m] = wo[:, pl.ds(pl.multiple_of(m * 256, 256), 256)]

    columns()
    returned(0).wait_recv()
    returned(1).wait_recv()

    def unpick(k):
        at = dcol[k * BLK:(k + 1) * BLK, :]
        got = jnp.zeros((BLK, 256), F32)
        for o in range(2):
            col = lax.broadcasted_iota(I32, (BLK, spans[o]), 1) + o * spans[0]
            pick = (col == at).astype(F32).astype(BF)
            got = got + jnp.dot(pick, backs[o][...], preferred_element_type=F32)
        G2[m, k] = got.astype(BF)

    def mix(k):
        if k == 0:
            for i in range(1, NMP):
                wcopy(i, lax.rem(m + NMP - i, NMP), lax.rem(m + i, NMP)).wait_recv()
        rows = jnp.concatenate([G2[i, k] for i in range(NMP)], axis=1)
        w = wcol[...].reshape(NMP * 256, 256)
        got = jnp.dot(rows, w, preferred_element_type=F32)
        out_ref[k * BLK:(k + 1) * BLK] = got.astype(BF)

    ring2 = Ring([(G2, k) for k in range(TOK // BLK)], s, m, ssem2, rsem2)
    for t in range(TOK // BLK + 3):
        ring2.step(t, unpick, mix)

    ring.drain()
    ring2.drain()
    for o, g in order:
        landed(o, g, bufs[o].at[g]).wait_send()
    whole(cnt.at[pl.ds(1, NSEQ - 1)], csend, crecv).wait_send()
    for o in range(2):
        returned(o).wait_send()
    for i in range(1, NMP):
        wcopy(i, m, lax.rem(m + i, NMP)).wait_send()


def layer(tokens, cluster_ids, w_query, w_value, w_out, caps, cid):
    vmem = pl.BlockSpec(memory_space=pltpu.VMEM)
    hbm = pl.BlockSpec(memory_space=pl.ANY)
    dma = pltpu.SemaphoreType.DMA
    spans = (NSEQ * caps[0], NSEQ * caps[1])
    chunks = TOK // BLK
    return pl.pallas_call(
        functools.partial(layer_kernel, caps=caps),
        out_shape=jax.ShapeDtypeStruct((TOK, 256), BF),
        in_specs=[vmem, vmem, vmem, hbm, hbm, hbm],
        out_specs=vmem,
        scratch_shapes=[
            pltpu.VMEM((2048, 256), BF),
            pltpu.VMEM((2048, 256), BF),
            pltpu.VMEM((256, 2048), BF),
            pltpu.VMEM((NMP, 256, 256), BF),
            pltpu.VMEM((GROUPS, 8 * caps[0], 256), BF),
            pltpu.VMEM((GROUPS, 8 * caps[1], 256), BF),
            pltpu.VMEM((NMP, GROUPS, 8 * caps[0], 256), BF),
            pltpu.VMEM((NMP, GROUPS, 8 * caps[1], 256), BF),
            pltpu.VMEM((spans[0], 256), BF),
            pltpu.VMEM((spans[1], 256), BF),
            pltpu.VMEM((spans[0], 512), BF),
            pltpu.VMEM((spans[1], 512), BF),
            pltpu.VMEM((8, spans[0]), F32),
            pltpu.VMEM((8, spans[1]), F32),
            pltpu.VMEM((spans[0], 256), BF),
            pltpu.VMEM((spans[1], 256), BF),
            pltpu.VMEM((spans[0], 256), BF),
            pltpu.VMEM((spans[1], 256), BF),
            pltpu.VMEM((NMP, chunks, BLK, 256), BF),
            pltpu.VMEM((NSEQ, 8, 128), F32),
            pltpu.VMEM((128, TOK), BF),
            pltpu.VMEM((1, TOK), I32),
            pltpu.VMEM((TOK, 1), I32),
            dma((3,)),
            dma((8, 2 * GROUPS)), dma((8, 2 * GROUPS)),
            dma((8, chunks)), dma((8, chunks)),
            dma((2 * GROUPS,)), dma((2 * GROUPS,)),
            dma, dma,
            dma((2,)), dma((2,)),
            dma((NMP,)), dma((NMP,)),
        ],
        compiler_params=pltpu.CompilerParams(
            collective_id=cid, has_side_effects=True, vmem_limit_bytes=60 * 1024 * 1024
        ),
        name="layer",
    )(tokens, cluster_ids.reshape(1, TOK), cluster_ids, w_query, w_value, w_out)


def shards(tokens, cluster_ids, w_query, w_value, w_out):
    return layer(tokens, cluster_ids, w_query, w_value, w_out, (CAP, CAP), 1)


def solution(mesh):
    return jax.shard_map(
        shards,
        mesh=mesh,
        in_specs=(P("seq", "mp"), P("seq", None), P(None, "mp"), P(None, "mp"), P("mp", None)),
        out_specs=P("seq", "mp"),
        check_vma=False,
    )
```

profile of v0, /device:TPU:1, one launch (start us, length us, event | category | flops | bytes accessed | tf_op | source)
XLA Modules:
  0.0 150.6 jit_solution(18109262946789241652)
XLA Ops:
  0.0 1.9 %copy.6.col_ref = s32[1536,1]{1,0:T(8,128)} copy(s32[1536,1]{0,1:T(1,128)} %param.6) | data formatting | bytes 12288 | tf_op args[1]
  1.9 146.6 %layer.1 = bf16[1536,256]{1,0:T(8,128)(2,1)} custom-call(bf16[1536,256]{1,0:T(8,128)(2,1)} %tok_ref.1, s32[1,1536]{1,0:T(1,128)} %bitcast.1, s32[1536,1]{1,0:T(8,128)} %copy.6.col_ref, bf16[2048,256]{1,0:T(8,128)(2,1)} %wq_hbm.1, bf16[2048,256]{1,0:T(8,128)(2,1)} %wv_hbm.1, bf16[256,2048]{1,0:T(8,128)(2,1)} %wo_hbm.1), custom_call_target="tpu_custom_call" | custom-call | tf_op jit(solution)/shard_map/layer/pallas_call | solution.py:416
  148.5 2.1 %copy.8 = bf16[1536,256]{1,0:T(8,128)(2,1)} copy(bf16[1536,256]{1,0:T(8,128)(2,1)} %layer.1) | data formatting | bytes 1572864
where the time goes:
time: 151 us
  Pallas kernels  147 us (97%)
  local copies, waits for them, and re-layouts  3.93 us (3%)
    pallas_call x1, Pallas kernels, layer(): pl.pallas_call(functools.partial(layer_kernel, caps=caps), out_shape=jax....  147 us
    unnamed x2, local copies, waits for them, and re-layouts  3.93 us

commit v1 on v0

v1 whole, which is shorter than its diff:
```python
import functools

import jax
import jax.numpy as jnp
import numpy as np
from jax import lax
from jax.experimental import pallas as pl
from jax.experimental.pallas import tpu as pltpu
from jax.sharding import PartitionSpec as P

HD = 128
CAP = 48
NZ, NY, NX = 8, 4, 4
NSEQ = NZ * NY
NMP = 2 * NX
TOK = 1536
BLK = 256
NEG = -1e30
MESH = pl.DeviceIdType.MESH
BF = jnp.bfloat16
F32 = jnp.float32
I32 = jnp.int32
FOLD = np.float32(1.4426950408889634 / np.sqrt(128.0))


def peer_of(s, r, sign):
    g, hi, dy = r // 8, (r // 4) % 2, r % 4
    minus = jnp.where(g == 0, 4, NZ - g)
    dz = jnp.where(hi == 0, g, minus)
    z, y = s // NY, s % NY
    return ((z + sign * dz + NZ) % NZ) * NY + (y + sign * dy + NY) % NY


def rank_of(cluster):
    return (cluster & 1) * NSEQ + (cluster >> 1)


def slot_of(s, src):
    dz = (s // NY - src // NY + NZ) % NZ
    hi = dz // 4
    g = (1 - hi) * dz + hi * ((NZ - dz) % 4)
    return g * 8 + hi * 4 + (s % NY - src % NY + NY) % NY


def first_row(rank, s, caps):
    z, y = s // NY, s % NY
    owner, o = rank & (NSEQ - 1), rank >> 5
    dz = ((owner >> 2) - z) & (NZ - 1)
    dy = ((owner & 3) - y) & (NY - 1)
    hi = dz >> 2
    g = jnp.where(hi == 1, (NZ - dz) & 3, dz)
    r = g * 8 + hi * 4 + dy
    return jnp.where(o == 0, r * caps[0], NSEQ * caps[0] + r * caps[1])


class Ring:
    def __init__(self, chunks, s, m, ssem, rsem):
        self.chunks, self.s, self.m = chunks, s, m
        self.ssem, self.rsem = ssem, rsem
        x, c = m // 2, m % 2
        self.right = ((x + 1) % NX) * 2 + c
        self.left = ((x + NX - 1) % NX) * 2 + c
        self.far = ((x + 2) % NX) * 2 + c
        self.sib = x * 2 + 1 - c

    def _copy(self, kind, k, block, to, half=None):
        G, p = self.chunks[k]
        ref = G.at[block, p]
        if half is not None:
            h = G.shape[2] // 2
            ref = G.at[block, p, pl.ds(half * h, h)]
        return pltpu.make_async_remote_copy(
            src_ref=ref,
            dst_ref=ref,
            send_sem=self.ssem.at[kind, k],
            recv_sem=self.rsem.at[kind, k],
            device_id=(self.s, to),
            device_id_type=MESH,
        )

    def send(self, i, k):
        block, to, half = (
            (self.m, self.right, None),
            (self.m, self.left, None),
            (self.m, self.sib, None),
            (self.left, self.right, 0),
            (self.right, self.left, 1),
            (self.left, self.sib, None),
            (self.right, self.sib, None),
            (self.far, self.sib, None),
        )[i]
        return self._copy(i, k, block, to, half)

    def arrival(self, i, k):
        other = lambda block: (block // 2) * 2 + 1 - block % 2
        block, half = (
            (self.left, None),
            (self.right, None),
            (self.sib, None),
            (self.far, 0),
            (self.far, 1),
            (other(self.left), None),
            (other(self.right), None),
            (other(self.far), None),
        )[i]
        return self._copy(i, k, block, self.sib, half)

    def own(self, k):
        for i in (0, 1, 2):
            self.send(i, k).start()

    def near(self, k):
        self.arrival(0, k).wait_recv()
        self.send(3, k).start()
        self.send(5, k).start()
        self.arrival(1, k).wait_recv()
        self.send(4, k).start()
        self.send(6, k).start()

    def across(self, k):
        self.arrival(3, k).wait_recv()
        self.arrival(4, k).wait_recv()
        self.send(7, k).start()

    def shared(self, k):
        for i in (2, 5, 6, 7):
            self.arrival(i, k).wait_recv()

    def drain(self):
        for k in range(len(self.chunks)):
            for i in range(8):
                self.send(i, k).wait_send()


def greet(s, m, mp_peers):
    barrier = pltpu.get_barrier_semaphore()

    def hello(r, carry):
        pl.semaphore_signal(
            barrier, inc=1, device_id=(peer_of(s, r, 1), m), device_id_type=MESH
        )
        return carry

    lax.fori_loop(1, NSEQ, hello, 0)
    for i in range(1, 1 + mp_peers):
        pl.semaphore_signal(
            barrier, inc=1, device_id=(s, lax.rem(m + i, NMP)), device_id_type=MESH
        )
    return barrier


def column(row, n):
    eye = lax.broadcasted_iota(I32, (n, n), 0) == lax.broadcasted_iota(I32, (n, n), 1)
    return jnp.sum(jnp.where(eye, row, 0.0), axis=1, keepdims=True)


def layer_kernel(
    tok_ref, row_ref, wq_hbm, wv_hbm, wo_hbm,
    out_ref,
    wq, wv, wo, wcol, buf0, buf1, G0, G1, q0, q1, v0, v1, have0, have1,
    att0, att1, back0, back1, G2, cnt, onehot, drow, dcol,
    lsem, ssem1, rsem1, ssem2, rsem2, dsend, drecv, csend, crecv,
    bsend, brecv, wsend, wrecv,
    *, caps, parts,
):
    s, m = lax.axis_index("seq"), lax.axis_index("mp")
    bufs, Gs, qs, vs = (buf0, buf1), (G0, G1), (q0, q1), (v0, v1)
    haves, atts, backs = (have0, have1), (att0, att1), (back0, back1)
    spans = (NSEQ * caps[0], NSEQ * caps[1])
    per = [NSEQ // n for n in parts]
    most = max(parts)

    loads = [
        pltpu.make_async_copy(a, b, lsem.at[i])
        for i, (a, b) in enumerate(((wq_hbm, wq), (wv_hbm, wv), (wo_hbm, wo)))
    ]
    for one in loads:
        one.start()

    barrier = greet(s, m, NMP - 1)

    i0 = lax.broadcasted_iota(I32, (BLK, BLK), 0)
    i1 = lax.broadcasted_iota(I32, (BLK, BLK), 1)
    upper = (i0 < i1).astype(F32).astype(BF)
    onehot[...] = (
        lax.broadcasted_iota(I32, (128, TOK), 0) == row_ref[...]
    ).astype(F32).astype(BF)
    rank = rank_of(lax.broadcasted_iota(I32, (1, 128), 1))
    seen = first_row(rank_of(lax.broadcasted_iota(I32, (128, 1), 0)), s, caps).astype(F32)
    for b in range(TOK // BLK):
        part = onehot[:, b * BLK:(b + 1) * BLK]
        wide = part.astype(F32)
        ahead = jnp.dot(part, upper, preferred_element_type=F32) + seen
        drow[:, b * BLK:(b + 1) * BLK] = jnp.sum(ahead * wide, axis=0, keepdims=True).astype(I32)
        seen = seen + jnp.sum(wide, axis=1, keepdims=True)
    pl.semaphore_wait(barrier, NSEQ - 1 + NMP - 1)

    def whole(ref, sem_s, sem_r):
        return pltpu.make_async_remote_copy(
            src_ref=ref, dst_ref=ref, send_sem=sem_s, recv_sem=sem_r,
            device_id=(s, m), device_id_type=MESH,
        )

    def block_copy(o, p, j):
        at = pl.ds(pl.multiple_of(j * caps[o], 16), caps[o])
        return pltpu.make_async_remote_copy(
            src_ref=bufs[o].at[p, at],
            dst_ref=Gs[o].at[m, p, at],
            send_sem=dsend.at[o * most + p],
            recv_sem=drecv.at[o * most + p],
            device_id=(peer_of(s, p * per[o] + j, 1), m),
            device_id_type=MESH,
        )

    def landed(o, p, ref):
        if p == 0:
            ref = ref.at[pl.ds(caps[o], (per[o] - 1) * caps[o])]
        return whole(ref, dsend.at[o * most + p], drecv.at[o * most + p])

    def scatter(o, p):
        n = per[o] * caps[o]
        row = lax.broadcasted_iota(I32, (n, TOK), 0) + (o * spans[0] + p * n)
        pick = (row == drow[...]).astype(F32).astype(BF)
        rows = jnp.dot(pick, tok_ref[...], preferred_element_type=F32).astype(BF)
        bufs[o][p] = rows
        if p == 0:
            Gs[o][m, 0, 0:caps[o]] = rows[0:caps[o]]

        def send(j, carry):
            block_copy(o, p, j).start()
            return carry

        lax.fori_loop(1 if p == 0 else 0, per[o], send, 0)

    turn = {2: (0, 1), 4: (1, 2, 3, 0), 8: (0, 2, 3, 4, 5, 6, 7, 1)}
    order = [(o, p) for o in range(2) for p in turn[parts[o]]]
    scattered = iter(order)

    def scatter_next(count):
        for _, (o, p) in zip(range(count), scattered):
            scatter(o, p)

    scatter_next(3)

    def ready(t):
        o, p = order[t]
        landed(o, p, Gs[o].at[m, p]).wait_recv()

    def project(k):
        o, p = order[k]
        if k == 0:
            loads[0].wait()
            loads[1].wait()
        cap = caps[o]
        rows = jnp.concatenate([Gs[o][i, p] for i in range(NMP)], axis=1)
        query = jnp.dot(rows, wq[...], preferred_element_type=F32).astype(BF)
        value = jnp.dot(rows, wv[...], preferred_element_type=F32).astype(BF)
        for j in range(per[o]):
            at = pl.ds(pl.multiple_of(peer_of(s, p * per[o] + j, -1) * cap, 16), cap)
            qs[o][at] = query[j * cap:(j + 1) * cap]
            for h in range(2):
                vs[o][at, h * 256:h * 256 + HD] = value[j * cap:(j + 1) * cap, h * HD:(h + 1) * HD]

    def tell_counts():
        cnt[0] = lax.dot_general(
            jnp.ones((8, TOK), BF), onehot[...], (((1,), (1,)), ((), ())),
            preferred_element_type=F32,
        )

        def send(r, carry):
            pltpu.make_async_remote_copy(
                src_ref=cnt.at[0], dst_ref=cnt.at[r], send_sem=csend, recv_sem=crecv,
                device_id=(peer_of(s, r, 1), m), device_id_type=MESH,
            ).start()
            return carry

        lax.fori_loop(1, NSEQ, send, 0)

    def counts():
        return whole(cnt.at[pl.ds(1, NSEQ - 1)], csend, crecv)

    def mark(o):
        have = jnp.where(rank == NSEQ * o + s, cnt[:, 0, :], 0.0)
        haves[o][...] = jnp.broadcast_to(jnp.sum(have, axis=1, keepdims=True), (NSEQ, HD))
        place = lax.broadcasted_iota(I32, (caps[o], HD), 0).astype(F32)

        def block(r, carry):
            at = pl.ds(pl.multiple_of(peer_of(s, r, -1) * caps[o], 16), caps[o])
            held = (place < haves[o][pl.ds(r, 1), :]).astype(F32).astype(BF)
            for h in range(2):
                vs[o][at, h * 256 + HD:(h + 1) * 256] = held
            return carry

        lax.fori_loop(0, NSEQ, block, 0)

    def columns():
        for b in range(TOK // BLK):
            at = slice(b * BLK, (b + 1) * BLK)
            dcol[at, :] = column(drow[:, at].astype(F32), BLK).astype(I32)

    def attend(o, i):
        lo, hi = i * BLK, (i + 1) * BLK
        dims = (((1,), (1,)), ((), ()))
        below = i0 >= i1
        for h in range(2):
            lanes = slice(h * HD, (h + 1) * HD)
            wide = slice(h * 256, (h + 1) * 256)
            query = qs[o][lo:hi, lanes]
            near = lax.dot_general(query, query, dims, preferred_element_type=F32) * FOLD
            near = jnp.where(below, near, NEG)
            top = jnp.max(near, axis=1, keepdims=True)
            if i:
                past = lax.dot_general(
                    query, qs[o][0:lo, lanes], dims, preferred_element_type=F32
                ) * FOLD
                top = jnp.maximum(top, jnp.max(past, axis=1, keepdims=True))
                got = jnp.dot(
                    jnp.exp2(past - top).astype(BF), vs[o][0:lo, wide],
                    preferred_element_type=F32,
                )
            expo = jnp.exp2(near - top).astype(BF)
            last = jnp.dot(expo, vs[o][lo:hi, wide], preferred_element_type=F32)
            got = got + last if i else last
            total = jnp.maximum(got[:, HD:], 0.5)
            atts[o][lo:hi, lanes] = (got[:, :HD] / total).astype(BF)

    def give_back(o, first, last):
        def send(at, carry):
            src = first + (at - first + s) % (last - first)
            r = slot_of(s, src)
            rows = pl.ds(pl.multiple_of(src * caps[o], 16), caps[o])

            @pl.when(src != s)
            def _():
                pltpu.make_async_remote_copy(
                    src_ref=atts[o].at[rows],
                    dst_ref=backs[o].at[pl.ds(pl.multiple_of(r * caps[o], 16), caps[o])],
                    send_sem=bsend.at[o],
                    recv_sem=brecv.at[o],
                    device_id=(src, m),
                    device_id_type=MESH,
                ).start()

            return carry

        lax.fori_loop(first, last, send, 0)

    def keep(o):
        backs[o][0:caps[o]] = atts[o][pl.ds(pl.multiple_of(s * caps[o], 16), caps[o])]

    def returned(o):
        ref = backs[o].at[pl.ds(caps[o], (NSEQ - 1) * caps[o])]
        return whole(ref, bsend.at[o], brecv.at[o])

    def pairs(o):
        half = spans[o] // BLK // 2
        ends = [(i + 1) * BLK // caps[o] for i in range(2 * half)]
        for i in range(half):
            yield i, ((ends[i - 1] if i else 0, ends[i]), (ends[i + half - 1], ends[i + half]))

    def attend_pair(o, i):
        half = spans[o] // BLK // 2
        for at, (first, last) in zip((i, i + half), dict(pairs(o))[i]):
            attend(o, at)
        for first, last in dict(pairs(o))[i]:
            give_back(o, first, last)
        if i == half - 1:
            keep(o)

    ring = Ring([(Gs[o], p) for o, p in order], s, m, ssem1, rsem1)

    def open_(k):
        ready(k)
        ring.own(k)

    def close(k):
        ring.shared(k)
        project(k)

    first, n = parts[0], len(order)
    half = spans[0] // BLK // 2
    for t in range(n + 3):
        if t < n:
            open_(t)
        scatter_next(2)
        if t == 2:
            tell_counts()
        if 3 <= t:
            close(t - 3)
        if 2 <= t < n + 2:
            ring.across(t - 2)
        if 1 <= t < n + 1:
            ring.near(t - 1)
        if t == first + 2:
            counts().wait_recv()
            mark(0)
        if first + 2 <= t < first + 2 + half:
            attend_pair(0, t - first - 2)
        if t == n:
            mark(1)
    for i in range(spans[1] // BLK // 2):
        attend_pair(1, i)

    loads[2].wait()

    def wcopy(i, block, to):
        return pltpu.make_async_remote_copy(
            src_ref=wo.at[:, pl.ds(pl.multiple_of(to * 256, 256), 256)],
            dst_ref=wcol.at[block],
            send_sem=wsend.at[i],
            recv_sem=wrecv.at[i],
            device_id=(s, to),
            device_id_type=MESH,
        )

    for i in range(1, NMP):
        wcopy(i, m, lax.rem(m + i, NMP)).start()
    wcol[m] = wo[:, pl.ds(pl.multiple_of(m * 256, 256), 256)]

    columns()
    returned(0).wait_recv()
    returned(1).wait_recv()

    def unpick(k):
        at = dcol[k * BLK:(k + 1) * BLK, :]
        got = jnp.zeros((BLK, 256), F32)
        for o in range(2):
            col = lax.broadcasted_iota(I32, (BLK, spans[o]), 1) + o * spans[0]
            pick = (col == at).astype(F32).astype(BF)
            got = got + jnp.dot(pick, backs[o][...], preferred_element_type=F32)
        G2[m, k] = got.astype(BF)

    def mix(k):
        if k == 0:
            for i in range(1, NMP):
                wcopy(i, lax.rem(m + NMP - i, NMP), lax.rem(m + i, NMP)).wait_recv()
        rows = jnp.concatenate([G2[i, k] for i in range(NMP)], axis=1)
        w = wcol[...].reshape(NMP * 256, 256)
        got = jnp.dot(rows, w, preferred_element_type=F32)
        out_ref[k * BLK:(k + 1) * BLK] = got.astype(BF)

    ring2 = Ring([(G2, k) for k in range(TOK // BLK)], s, m, ssem2, rsem2)
    n = TOK // BLK
    for t in range(n + 3):
        if t < n:
            unpick(t)
            ring2.own(t)
        if 3 <= t:
            ring2.shared(t - 3)
            mix(t - 3)
        if 2 <= t < n + 2:
            ring2.across(t - 2)
        if 1 <= t < n + 1:
            ring2.near(t - 1)

    ring.drain()
    ring2.drain()
    for o, p in order:
        landed(o, p, bufs[o].at[p]).wait_send()
    counts().wait_send()
    for o in range(2):
        returned(o).wait_send()
    for i in range(1, NMP):
        wcopy(i, m, lax.rem(m + i, NMP)).wait_send()


def layer(tokens, ids, w_query, w_value, w_out, caps, parts, cid):
    vmem = pl.BlockSpec(memory_space=pltpu.VMEM)
    hbm = pl.BlockSpec(memory_space=pl.ANY)
    dma = pltpu.SemaphoreType.DMA
    spans = (NSEQ * caps[0], NSEQ * caps[1])
    chunks, most = TOK // BLK, max(parts)
    buf = [pltpu.VMEM((n, span // n, 256), BF) for n, span in zip(parts, spans)]
    G = [pltpu.VMEM((NMP, n, span // n, 256), BF) for n, span in zip(parts, spans)]
    flat = [pltpu.VMEM((span, 256), BF) for span in spans]
    return pl.pallas_call(
        functools.partial(layer_kernel, caps=caps, parts=parts),
        out_shape=jax.ShapeDtypeStruct((TOK, 256), BF),
        in_specs=[vmem] * 2 + [hbm] * 3,
        out_specs=vmem,
        scratch_shapes=[
            pltpu.VMEM((2048, 256), BF),
            pltpu.VMEM((2048, 256), BF),
            pltpu.VMEM((256, 2048), BF),
            pltpu.VMEM((NMP, 256, 256), BF),
            *buf,
            *G,
            *flat,
            *[pltpu.VMEM((span, 512), BF) for span in spans],
            *[pltpu.VMEM((NSEQ, HD), F32)] * 2,
            *flat,
            *flat,
            pltpu.VMEM((NMP, chunks, BLK, 256), BF),
            pltpu.VMEM((NSEQ, 8, 128), F32),
            pltpu.VMEM((128, TOK), BF),
            pltpu.VMEM((1, TOK), I32),
            pltpu.VMEM((TOK, 1), I32),
            dma((3,)),
            dma((8, sum(parts))), dma((8, sum(parts))),
            dma((8, chunks)), dma((8, chunks)),
            dma((2 * most,)), dma((2 * most,)),
            dma, dma,
            dma((2,)), dma((2,)),
            dma((NMP,)), dma((NMP,)),
        ],
        compiler_params=pltpu.CompilerParams(
            collective_id=cid, has_side_effects=True, vmem_limit_bytes=60 * 1024 * 1024
        ),
        name="layer",
    )(tokens, ids, w_query, w_value, w_out)


def shards(tokens, cluster_ids, w_query, w_value, w_out):
    ids = cluster_ids.reshape(1, TOK)
    return layer(tokens, ids, w_query, w_value, w_out, (CAP, CAP), (4, 4), 1)


def solution(mesh):
    return jax.shard_map(
        shards,
        mesh=mesh,
        in_specs=(P("seq", "mp"), P("seq", None), P(None, "mp"), P(None, "mp"), P("mp", None)),
        out_specs=P("seq", "mp"),
        check_vma=False,
    )
```

time: 151 us -> 138 us (0.914)
  the two profiles are of different devices: /device:TPU:1 before, /device:TPU:97 now
where the time goes in v1:
time: 138 us; the launch traced here: 137 us
  Pallas kernels  135 us (98%)
  local copies, waits for them, and re-layouts  2.06 us (1%)
    pallas_call x1, Pallas kernels, layer(): pl.pallas_call(functools.partial(layer_kernel, caps=caps, parts=parts), o...  135 us

profile of v1, /device:TPU:97, one launch (start us, length us, event | category | flops | bytes accessed | tf_op | source)
XLA Modules:
  0.0 136.9 jit_solution(1242076847775809259)
XLA Ops:
  0.0 134.8 %layer.1 = bf16[1536,256]{1,0:T(8,128)(2,1)} custom-call(bf16[1536,256]{1,0:T(8,128)(2,1)} %tok_ref.1, s32[1,1536]{1,0:T(1,128)} %bitcast.1, bf16[2048,256]{1,0:T(8,128)(2,1)} %wq_hbm.1, bf16[2048,256]{1,0:T(8,128)(2,1)} %wv_hbm.1, bf16[256,2048]{1,0:T(8,128)(2,1)} %wo_hbm.1), custom_call_target="tpu_custom_call" | custom-call | tf_op jit(solution)/shard_map/layer/pallas_call | solution.py:476
  134.8 2.1 %copy.7 = bf16[1536,256]{1,0:T(8,128)(2,1)} copy(bf16[1536,256]{1,0:T(8,128)(2,1)} %layer.1) | data formatting | bytes 1572864

commit v2 on v1

--- a/solution.py
+++ b/solution.py
@@ -15,6 +15,10 @@
 NMP = 2 * NX
 TOK = 1536
 BLK = 256
+ROWS = 256
+AHEAD = 1
+FIRST = ((0, 4), (8, 8), (16, 8), (24, 8), (4, 4))
+SECOND = ((8, 8), (16, 8), (24, 8), (0, 8))
 NEG = -1e30
 MESH = pl.DeviceIdType.MESH
 BF = jnp.bfloat16
@@ -64,11 +68,11 @@
         self.sib = x * 2 + 1 - c
 
     def _copy(self, kind, k, block, to, half=None):
-        G, p = self.chunks[k]
-        ref = G.at[block, p]
+        G, start, rows = self.chunks[k]
         if half is not None:
-            h = G.shape[2] // 2
-            ref = G.at[block, p, pl.ds(half * h, h)]
+            rows = rows // 2
+            start = start + half * rows
+        ref = G.at[block, pl.ds(start, rows)]
         return pltpu.make_async_remote_copy(
             src_ref=ref,
             dst_ref=ref,
@@ -155,9 +159,9 @@
 
 
 def layer_kernel(
-    tok_ref, row_ref, wq_hbm, wv_hbm, wo_hbm,
+    row_ref, tok_hbm, wq_hbm, wv_hbm, wo_hbm,
     out_ref,
-    wq, wv, wo, wcol, buf0, buf1, G0, G1, q0, q1, v0, v1, have0, have1,
+    tok_ref, wq, wv, wo, wcol, buf0, buf1, G0, G1, q0, q1, v0, v1, have0, have1,
     att0, att1, back0, back1, G2, cnt, onehot, drow, dcol,
     lsem, ssem1, rsem1, ssem2, rsem2, dsend, drecv, csend, crecv,
     bsend, brecv, wsend, wrecv,
@@ -167,17 +171,16 @@
     bufs, Gs, qs, vs = (buf0, buf1), (G0, G1), (q0, q1), (v0, v1)
     haves, atts, backs = (have0, have1), (att0, att1), (back0, back1)
     spans = (NSEQ * caps[0], NSEQ * caps[1])
-    per = [NSEQ // n for n in parts]
-    most = max(parts)
 
     loads = [
         pltpu.make_async_copy(a, b, lsem.at[i])
-        for i, (a, b) in enumerate(((wq_hbm, wq), (wv_hbm, wv), (wo_hbm, wo)))
+        for i, (a, b) in enumerate(
+            ((wq_hbm, wq), (wv_hbm, wv), (wo_hbm, wo), (tok_hbm, tok_ref))
+        )
     ]
-    for one in loads:
-        one.start()
-
     barrier = greet(s, m, NMP - 1)
+    for i in (3, 0, 1, 2):
+        loads[i].start()
 
     i0 = lax.broadcasted_iota(I32, (BLK, BLK), 0)
     i1 = lax.broadcasted_iota(I32, (BLK, BLK), 1)
@@ -201,62 +204,69 @@
             device_id=(s, m), device_id_type=MESH,
         )
 
-    def block_copy(o, p, j):
-        at = pl.ds(pl.multiple_of(j * caps[o], 16), caps[o])
+    def block_copy(k, r):
+        o = order[k][0]
+        at = pl.ds(pl.multiple_of(r * caps[o], 16), caps[o])
         return pltpu.make_async_remote_copy(
-            src_ref=bufs[o].at[p, at],
-            dst_ref=Gs[o].at[m, p, at],
-            send_sem=dsend.at[o * most + p],
-            recv_sem=drecv.at[o * most + p],
-            device_id=(peer_of(s, p * per[o] + j, 1), m),
+            src_ref=bufs[o].at[at],
+            dst_ref=Gs[o].at[m, at],
+            send_sem=dsend.at[k],
+            recv_sem=drecv.at[k],
+            device_id=(peer_of(s, r, 1), m),
             device_id_type=MESH,
         )
 
-    def landed(o, p, ref):
-        if p == 0:
-            ref = ref.at[pl.ds(caps[o], (per[o] - 1) * caps[o])]
-        return whole(ref, dsend.at[o * most + p], drecv.at[o * most + p])
-
-    def scatter(o, p):
-        n = per[o] * caps[o]
-        row = lax.broadcasted_iota(I32, (n, TOK), 0) + (o * spans[0] + p * n)
+    def rows_of(k):
+        o, r, n = order[k]
+        return r * caps[o], n * caps[o]
+
+    def landed(k, ref):
+        start, rows = rows_of(k)
+        if start == 0:
+            start, rows = caps[order[k][0]], rows - caps[order[k][0]]
+        return whole(ref.at[pl.ds(start, rows)], dsend.at[k], drecv.at[k])
+
+    def scatter(k):
+        o, r, n = order[k]
+        start, rows = rows_of(k)
+        row = lax.broadcasted_iota(I32, (rows, TOK), 0) + (o * spans[0] + start)
         pick = (row == drow[...]).astype(F32).astype(BF)
-        rows = jnp.dot(pick, tok_ref[...], preferred_element_type=F32).astype(BF)
-        bufs[o][p] = rows
-        if p == 0:
-            Gs[o][m, 0, 0:caps[o]] = rows[0:caps[o]]
-
-        def send(j, carry):
-            block_copy(o, p, j).start()
+        got = jnp.dot(pick, tok_ref[...], preferred_element_type=F32).astype(BF)
+        bufs[o][start:start + rows] = got
+        if r == 0:
+            Gs[o][m, 0:caps[o]] = got[0:caps[o]]
+
+        def send(at, carry):
+            block_copy(k, at).start()
             return carry
 
-        lax.fori_loop(1 if p == 0 else 0, per[o], send, 0)
-
-    turn = {2: (0, 1), 4: (1, 2, 3, 0), 8: (0, 2, 3, 4, 5, 6, 7, 1)}
-    order = [(o, p) for o in range(2) for p in turn[parts[o]]]
-    scattered = iter(order)
+        lax.fori_loop(max(r, 1), r + n, send, 0)
+
+    order = [(o, r, n) for o in range(2) for r, n in parts[o]]
+    scattered = iter(range(len(order)))
 
     def scatter_next(count):
-        for _, (o, p) in zip(range(count), scattered):
-            scatter(o, p)
-
+        for _, k in zip(range(count), scattered):
+            scatter(k)
+
+    loads[3].wait()
     scatter_next(3)
 
     def ready(t):
-        o, p = order[t]
-        landed(o, p, Gs[o].at[m, p]).wait_recv()
+        landed(t, Gs[order[t][0]].at[m]).wait_recv()
 
     def project(k):
-        o, p = order[k]
+        o, r, n = order[k]
+        start, size = rows_of(k)
         if k == 0:
             loads[0].wait()
             loads[1].wait()
         cap = caps[o]
-        rows = jnp.concatenate([Gs[o][i, p] for i in range(NMP)], axis=1)
+        rows = jnp.concatenate([Gs[o][i, start:start + size] for i in range(NMP)], axis=1)
         query = jnp.dot(rows, wq[...], preferred_element_type=F32).astype(BF)
         value = jnp.dot(rows, wv[...], preferred_element_type=F32).astype(BF)
-        for j in range(per[o]):
-            at = pl.ds(pl.multiple_of(peer_of(s, p * per[o] + j, -1) * cap, 16), cap)
+        for j in range(n):
+            at = pl.ds(pl.multiple_of(peer_of(s, r + j, -1) * cap, 16), cap)
             qs[o][at] = query[j * cap:(j + 1) * cap]
             for h in range(2):
                 vs[o][at, h * 256:h * 256 + HD] = value[j * cap:(j + 1) * cap, h * HD:(h + 1) * HD]
@@ -367,7 +377,7 @@
         if i == half - 1:
             keep(o)
 
-    ring = Ring([(Gs[o], p) for o, p in order], s, m, ssem1, rsem1)
+    ring = Ring([(Gs[order[k][0]], *rows_of(k)) for k in range(len(order))], s, m, ssem1, rsem1)
 
     def open_(k):
         ready(k)
@@ -377,7 +387,7 @@
         ring.shared(k)
         project(k)
 
-    first, n = parts[0], len(order)
+    first, n = len(parts[0]), len(order)
     half = spans[0] // BLK // 2
     for t in range(n + 3):
         if t < n:
@@ -417,34 +427,42 @@
         wcopy(i, m, lax.rem(m + i, NMP)).start()
     wcol[m] = wo[:, pl.ds(pl.multiple_of(m * 256, 256), 256)]
 
+    def unpick(k, o):
+        at = dcol[k * ROWS:(k + 1) * ROWS, :]
+        col = lax.broadcasted_iota(I32, (ROWS, spans[o]), 1) + o * spans[0]
+        pick = (col == at).astype(F32).astype(BF)
+        got = jnp.dot(pick, backs[o][...], preferred_element_type=F32).astype(BF)
+        at = slice(k * ROWS, (k + 1) * ROWS)
+        G2[m, at] = got if o == 0 else got + G2[m, at]
+
+    n = TOK // ROWS
     columns()
     returned(0).wait_recv()
+    for k in range(n):
+        unpick(k, 0)
     returned(1).wait_recv()
-
-    def unpick(k):
-        at = dcol[k * BLK:(k + 1) * BLK, :]
-        got = jnp.zeros((BLK, 256), F32)
-        for o in range(2):
-            col = lax.broadcasted_iota(I32, (BLK, spans[o]), 1) + o * spans[0]
-            pick = (col == at).astype(F32).astype(BF)
-            got = got + jnp.dot(pick, backs[o][...], preferred_element_type=F32)
-        G2[m, k] = got.astype(BF)
 
     def mix(k):
         if k == 0:
             for i in range(1, NMP):
                 wcopy(i, lax.rem(m + NMP - i, NMP), lax.rem(m + i, NMP)).wait_recv()
-        rows = jnp.concatenate([G2[i, k] for i in range(NMP)], axis=1)
+        rows = jnp.concatenate(
+            [G2[i, k * ROWS:(k + 1) * ROWS] for i in range(NMP)], axis=1
+        )
         w = wcol[...].reshape(NMP * 256, 256)
         got = jnp.dot(rows, w, preferred_element_type=F32)
-        out_ref[k * BLK:(k + 1) * BLK] = got.astype(BF)
-
-    ring2 = Ring([(G2, k) for k in range(TOK // BLK)], s, m, ssem2, rsem2)
-    n = TOK // BLK
-    for t in range(n + 3):
-        if t < n:
-            unpick(t)
-            ring2.own(t)
+        out_ref[k * ROWS:(k + 1) * ROWS] = got.astype(BF)
+
+    ring2 = Ring([(G2, k * ROWS, ROWS) for k in range(n)], s, m, ssem2, rsem2)
+    def send_own(k):
+        if k < n:
+            unpick(k, 1)
+            ring2.own(k)
+
+    for k in range(AHEAD):
+        send_own(k)
+    for t in range(1, n + 3):
+        send_own(t + AHEAD - 1)
         if 3 <= t:
             ring2.shared(t - 3)
             mix(t - 3)
@@ -455,8 +473,8 @@
 
     ring.drain()
     ring2.drain()
-    for o, p in order:
-        landed(o, p, bufs[o].at[p]).wait_send()
+    for k in range(len(order)):
+        landed(k, bufs[order[k][0]]).wait_send()
     counts().wait_send()
     for o in range(2):
         returned(o).wait_send()
@@ -469,36 +487,36 @@
     hbm = pl.BlockSpec(memory_space=pl.ANY)
     dma = pltpu.SemaphoreType.DMA
     spans = (NSEQ * caps[0], NSEQ * caps[1])
-    chunks, most = TOK // BLK, max(parts)
-    buf = [pltpu.VMEM((n, span // n, 256), BF) for n, span in zip(parts, spans)]
-    G = [pltpu.VMEM((NMP, n, span // n, 256), BF) for n, span in zip(parts, spans)]
+    chunks, total = TOK // ROWS, sum(len(one) for one in parts)
+    G = [pltpu.VMEM((NMP, span, 256), BF) for span in spans]
     flat = [pltpu.VMEM((span, 256), BF) for span in spans]
     return pl.pallas_call(
         functools.partial(layer_kernel, caps=caps, parts=parts),
         out_shape=jax.ShapeDtypeStruct((TOK, 256), BF),
-        in_specs=[vmem] * 2 + [hbm] * 3,
+        in_specs=[vmem] + [hbm] * 4,
         out_specs=vmem,
         scratch_shapes=[
+            pltpu.VMEM((TOK, 256), BF),
             pltpu.VMEM((2048, 256), BF),
             pltpu.VMEM((2048, 256), BF),
             pltpu.VMEM((256, 2048), BF),
             pltpu.VMEM((NMP, 256, 256), BF),
-            *buf,
+            *flat,
             *G,
             *flat,
             *[pltpu.VMEM((span, 512), BF) for span in spans],
             *[pltpu.VMEM((NSEQ, HD), F32)] * 2,
             *flat,
             *flat,
-            pltpu.VMEM((NMP, chunks, BLK, 256), BF),
+            pltpu.VMEM((NMP, TOK, 256), BF),
             pltpu.VMEM((NSEQ, 8, 128), F32),
             pltpu.VMEM((128, TOK), BF),
             pltpu.VMEM((1, TOK), I32),
             pltpu.VMEM((TOK, 1), I32),
-            dma((3,)),
-            dma((8, sum(parts))), dma((8, sum(parts))),
+            dma((4,)),
+            dma((8, total)), dma((8, total)),
             dma((8, chunks)), dma((8, chunks)),
-            dma((2 * most,)), dma((2 * most,)),
+            dma((total,)), dma((total,)),
             dma, dma,
             dma((2,)), dma((2,)),
             dma((NMP,)), dma((NMP,)),
@@ -507,12 +525,12 @@
             collective_id=cid, has_side_effects=True, vmem_limit_bytes=60 * 1024 * 1024
         ),
         name="layer",
-    )(tokens, ids, w_query, w_value, w_out)
+    )(ids, tokens, w_query, w_value, w_out)
 
 
 def shards(tokens, cluster_ids, w_query, w_value, w_out):
     ids = cluster_ids.reshape(1, TOK)
-    return layer(tokens, ids, w_query, w_value, w_out, (CAP, CAP), (4, 4), 1)
+    return layer(tokens, ids, w_query, w_value, w_out, (CAP, CAP), (FIRST, SECOND), 1)
 
 
 def solution(mesh):

time: 138 us -> 135 us (0.978)
  Pallas kernels: 135 us -> 132 us
    pallas_call x1, Pallas kernels: 135 us -> 132 us  [layer(): pl.pallas_call(functools.partial(layer_kernel, caps=caps, parts=parts), o...]
where the time goes in v2:
time: 135 us; the launch traced here: 134 us
  Pallas kernels  132 us (98%)
  local copies, waits for them, and re-layouts  2.06 us (2%)
    pallas_call x1, Pallas kernels, layer(): pl.pallas_call(functools.partial(layer_kernel, caps=caps, parts=parts), o...  132 us

profile of v2, /device:TPU:97, one launch (start us, length us, event | category | flops | bytes accessed | tf_op | source)
XLA Modules:
  0.0 134.5 jit_solution(8350573377113347380)
XLA Ops:
  0.0 132.4 %layer.1 = bf16[1536,256]{1,0:T(8,128)(2,1)} custom-call(s32[1,1536]{1,0:T(1,128)} %bitcast.1, bf16[1536,256]{1,0:T(8,128)(2,1)} %tok_hbm.1, bf16[2048,256]{1,0:T(8,128)(2,1)} %wq_hbm.1, bf16[2048,256]{1,0:T(8,128)(2,1)} %wv_hbm.1, bf16[256,2048]{1,0:T(8,128)(2,1)} %wo_hbm.1), custom_call_target="tpu_custom_call" | custom-call | tf_op jit(solution)/shard_map/layer/pallas_call | solution.py:493
  132.4 2.1 %copy.7 = bf16[1536,256]{1,0:T(8,128)(2,1)} copy(bf16[1536,256]{1,0:T(8,128)(2,1)} %layer.1) | data formatting | bytes 1572864

commit v3 on v2

--- a/solution.py
+++ b/solution.py
@@ -15,7 +15,7 @@
 NMP = 2 * NX
 TOK = 1536
 BLK = 256
-ROWS = 256
+ROWS = 384
 AHEAD = 1
 FIRST = ((0, 4), (8, 8), (16, 8), (24, 8), (4, 4))
 SECOND = ((8, 8), (16, 8), (24, 8), (0, 8))
@@ -250,7 +250,7 @@
             scatter(k)
 
     loads[3].wait()
-    scatter_next(3)
+    scatter_next(5)
 
     def ready(t):
         landed(t, Gs[order[t][0]].at[m]).wait_recv()
@@ -404,9 +404,10 @@
         if t == first + 2:
             counts().wait_recv()
             mark(0)
-        if first + 2 <= t < first + 2 + half:
-            attend_pair(0, t - first - 2)
-        if t == n:
+            for i in range(half - 1):
+                attend_pair(0, i)
+        if t == first + 3:
+            attend_pair(0, half - 1)
             mark(1)
     for i in range(spans[1] // BLK // 2):
         attend_pair(1, i)

time: 135 us -> 134 us (level)
  no operation moved by 1% of the time
where the time goes in v3:
time: 134 us
  Pallas kernels  132 us (99%)
  local copies, waits for them, and re-layouts  2.06 us (2%)
    pallas_call x1, Pallas kernels, layer(): pl.pallas_call(functools.partial(layer_kernel, caps=caps, parts=parts), o...  132 us

profile of v3, /device:TPU:97, one launch (start us, length us, event | category | flops | bytes accessed | tf_op | source)
XLA Modules:
  0.0 133.6 jit_solution(15200678083576964255)
XLA Ops:
  0.0 131.6 %layer.1 = bf16[1536,256]{1,0:T(8,128)(2,1)} custom-call(s32[1,1536]{1,0:T(1,128)} %bitcast.1, bf16[1536,256]{1,0:T(8,128)(2,1)} %tok_hbm.1, bf16[2048,256]{1,0:T(8,128)(2,1)} %wq_hbm.1, bf16[2048,256]{1,0:T(8,128)(2,1)} %wv_hbm.1, bf16[256,2048]{1,0:T(8,128)(2,1)} %wo_hbm.1), custom_call_target="tpu_custom_call" | custom-call | tf_op jit(solution)/shard_map/layer/pallas_call | solution.py:494
  131.6 2.1 %copy.7 = bf16[1536,256]{1,0:T(8,128)(2,1)} copy(bf16[1536,256]{1,0:T(8,128)(2,1)} %layer.1) | data formatting | bytes 1572864

commit v4 on v3

--- a/solution.py
+++ b/solution.py
@@ -160,8 +160,8 @@
 
 def layer_kernel(
     row_ref, tok_hbm, wq_hbm, wv_hbm, wo_hbm,
-    out_ref,
-    tok_ref, wq, wv, wo, wcol, buf0, buf1, G0, G1, q0, q1, v0, v1, have0, have1,
+    out_hbm,
+    out_ref, osem, tok_ref, wq, wv, wo, wcol, buf0, buf1, G0, G1, q0, q1, v0, v1, have0, have1,
     att0, att1, back0, back1, G2, cnt, onehot, drow, dcol,
     lsem, ssem1, rsem1, ssem2, rsem2, dsend, drecv, csend, crecv,
     bsend, brecv, wsend, wrecv,
@@ -443,6 +443,10 @@
         unpick(k, 0)
     returned(1).wait_recv()
 
+    def store(k):
+        at = pl.ds(k * ROWS, ROWS)
+        return pltpu.make_async_copy(out_ref.at[at], out_hbm.at[at], osem.at[k])
+
     def mix(k):
         if k == 0:
             for i in range(1, NMP):
@@ -453,6 +457,7 @@
         w = wcol[...].reshape(NMP * 256, 256)
         got = jnp.dot(rows, w, preferred_element_type=F32)
         out_ref[k * ROWS:(k + 1) * ROWS] = got.astype(BF)
+        store(k).start()
 
     ring2 = Ring([(G2, k * ROWS, ROWS) for k in range(n)], s, m, ssem2, rsem2)
     def send_own(k):
@@ -472,6 +477,8 @@
         if 1 <= t < n + 1:
             ring2.near(t - 1)
 
+    for k in range(n):
+        store(k).wait()
     ring.drain()
     ring2.drain()
     for k in range(len(order)):
@@ -495,8 +502,10 @@
         functools.partial(layer_kernel, caps=caps, parts=parts),
         out_shape=jax.ShapeDtypeStruct((TOK, 256), BF),
         in_specs=[vmem] + [hbm] * 4,
-        out_specs=vmem,
+        out_specs=hbm,
         scratch_shapes=[
+            pltpu.VMEM((TOK, 256), BF),
+            dma((chunks,)),
             pltpu.VMEM((TOK, 256), BF),
             pltpu.VMEM((2048, 256), BF),
             pltpu.VMEM((2048, 256), BF),

time: 134 us -> 134 us (level)
  no operation moved by 1% of the time
where the time goes in v4:
time: 134 us; the launch traced here: 133 us
  Pallas kernels  131 us (98%)
  local copies, waits for them, and re-layouts  2.06 us (2%)
    pallas_call x1, Pallas kernels, layer(): pl.pallas_call(functools.partial(layer_kernel, caps=caps, parts=parts), o...  131 us

profile of v4, /device:TPU:97, one launch (start us, length us, event | category | flops | bytes accessed | tf_op | source)
XLA Modules:
  0.0 133.5 jit_solution(607084514893830145)
XLA Ops:
  0.0 131.4 %layer.1 = bf16[1536,256]{1,0:T(8,128)(2,1)} custom-call(s32[1,1536]{1,0:T(1,128)} %bitcast.1, bf16[1536,256]{1,0:T(8,128)(2,1)} %tok_hbm.1, bf16[2048,256]{1,0:T(8,128)(2,1)} %wq_hbm.1, bf16[2048,256]{1,0:T(8,128)(2,1)} %wv_hbm.1, bf16[256,2048]{1,0:T(8,128)(2,1)} %wo_hbm.1), custom_call_target="tpu_custom_call" | custom-call | tf_op jit(solution)/shard_map/layer/pallas_call | solution.py:501
  131.4 2.1 %copy.7 = bf16[1536,256]{1,0:T(8,128)(2,1)} copy(bf16[1536,256]{1,0:T(8,128)(2,1)} %layer.1) | data formatting | bytes 1572864
